TPU v7x, 512 devices: a whole 4x4x16 slice. The times are simulated.
512 devices in a mesh: sub: 32 (over z, core), blk: 16 (over y, x).
Axes of the slice: x: 4, y: 4, z: 16, core: 2. Of those that a mesh axis runs over, the one named last changes fastest.
Arguments:
- impedance: bfloat16 [32, 16384, 1024], P('sub', 'blk'), may hold values from -0.1875 to 0.1875
- port_node: int32 [32, 1024], P('sub', 'blk'), may hold values from 0 to 16383, as said below
- far_system: int32 [32, 1024], P('sub', 'blk'), may hold values from 0 to 31, as said below
- delays: int32 [32, 1024], P('sub', 'blk'), may hold values from 2 to 4, as said below
- admittance: float32 [32, 1024], P('sub', 'blk'), may hold values from 0.5 to 2
- pole_rates: float32 [32, 12, 1024], P('sub', None, 'blk'), may hold values from 0.05 to 0.95
- residues: float32 [32, 12, 1024], P('sub', None, 'blk'), may hold values from -1.8 to 1.8
- states: float32 [32, 12, 1024, 256], P('sub', None, 'blk'), may hold values from -3 to 3
- history: float32 [32, 4, 1024, 256], P('sub', None, 'blk'), may hold values from -6 to 6
- event_port: int32 [32, 256], P('sub'), may hold values from 0 to 1023
- amplitude: float32 [32, 2, 256], P('sub'), may hold values from -48 to 48
Outputs:
- peak_voltage: bfloat16 [32, 16384, 256], P('sub', 'blk')
- new_states: float32 [32, 12, 1024, 256], P('sub', None, 'blk')
- arrived: float32 [32, 1024, 2, 256], P('sub', 'blk')
Inputs may be any that keep to these rules, and one draw needn't show every extreme that they name: `port_node`: the node of terminal j lies in rows (j // 64) * 1024 to (j // 64 + 1) * 1024 - 1; the terminals of one subsystem have distinct nodes. Line j joins terminal j of two different subsystems: far_system[far_system[s, j], j] = s and far_system[s, j] != s. Of the terminals b * 64 to (b + 1) * 64 - 1 of one subsystem at most 6 lead to one same subsystem, and in every such group exactly 6 do for one of them. delays[s, j] = delays[far_system[s, j], j].
All inputs are finite; a program needn't handle non-finite values.
Results may differ from a plain program's by a relative error of at most 0.0042.
Values may be sent and summed in bfloat16 or wider, within the bound.
A program may use at most 64 MiB of HBM per device.

v0:
```python
import jax
import jax.numpy as jnp
from jax import lax
from jax.sharding import PartitionSpec as P


def pick_incident(history, delays, step_index):
    depth_iota = jnp.arange(history.shape[0], dtype=jnp.int32)
    wanted = delays - step_index - 1
    chosen = jnp.where(wanted[None, :, None] == depth_iota[:, None, None], history, 0.0)
    return jnp.sum(chosen, axis=0)


def deliver(emitted, partners):
    port_count = partners.shape[0]
    columns = emitted.shape[1]
    local_index = jnp.arange(port_count, dtype=jnp.int32)
    earlier = local_index[:, None] > local_index[None, :]
    slot_ranks = jnp.sum(jnp.logical_and(partners[:, None] == partners[None, :], earlier), axis=1)
    systems = lax.axis_size("sub")
    surplus = max(1, port_count // 16)
    capacity = (port_count - surplus + systems - 2) // (systems - 1) + surplus
    slot_rows = partners * capacity + slot_ranks
    outbox = jnp.zeros((systems * capacity, columns), jnp.float32).at[slot_rows].set(emitted)
    received = lax.all_to_all(
        outbox.reshape(systems, capacity, columns), "sub", split_axis=0, concat_axis=0, tiled=True
    )
    return received.reshape(systems * capacity, columns)[slot_rows]


def body(
    impedance,
    port_node,
    far_system,
    delays,
    admittance,
    pole_rates,
    residues,
    states,
    history,
    event_port,
    amplitude,
):
    node_rows = impedance.shape[1]
    port_count = port_node.shape[1]
    scenarios = states.shape[3]
    steps_total = amplitude.shape[1]
    block_index = lax.axis_index("blk")
    port_index = block_index * port_count + jnp.arange(port_count, dtype=jnp.int32)
    local_nodes = port_node[0] - block_index * node_rows
    matrix = impedance[0]
    decay_rates = pole_rates[0][:, :, None]
    weights = residues[0][:, :, None]
    partners = far_system[0]
    line_admittance = admittance[0][:, None]
    current = states[0]
    sources = []
    injections = []
    for step_index in range(steps_total):
        incident = pick_incident(history[0], delays[0], step_index)
        current = decay_rates * current + weights * incident[None]
        source = jnp.sum(current, axis=0)
        switched = jnp.where(
            event_port[0][None, :] == port_index[:, None], amplitude[0, step_index][None, :], 0.0
        )
        sources.append(source)
        injections.append((source + switched).astype(jnp.bfloat16))
    voltages = []
    arrivals = []
    for step_index in range(steps_total):
        voltage = jnp.dot(
            matrix,
            lax.all_gather(injections[step_index], "blk", axis=0, tiled=True),
            preferred_element_type=jnp.float32,
        )
        voltages.append(voltage)
        emitted_now = 2.0 * line_admittance * voltage[local_nodes] - sources[step_index]
        arrivals.append(deliver(emitted_now, partners))
    arrived = jnp.stack(arrivals, axis=1)
    peak_value = jnp.zeros((node_rows, scenarios), jnp.float32)
    for voltage in voltages:
        peak_value = jnp.maximum(peak_value, jnp.abs(voltage))
    return (peak_value.astype(jnp.bfloat16)[None], current[None], arrived[None])


def solution(mesh):
    placed = (
        P("sub", "blk", None),
        P("sub", "blk"),
        P("sub", "blk"),
        P("sub", "blk"),
        P("sub", "blk"),
        P("sub", None, "blk"),
        P("sub", None, "blk"),
        P("sub", None, "blk", None),
        P("sub", None, "blk", None),
        P("sub", None),
        P("sub", None, None),
    )
    return jax.shard_map(
        body,
        mesh=mesh,
        in_specs=placed,
        out_specs=(P("sub", "blk", None), P("sub", None, "blk", None), P("sub", "blk", None, None)),
        check_vma=False,
    )
```

profile of v0, /device:TPU:1, one launch (start us, length us, event | category | flops | bytes accessed | tf_op | source)
XLA Modules:
  0.0 123.7 jit_solution(7459575699059238528)
XLA Ops:
  0.6 0.0 copy-start
  0.6 0.8 add_bitcast_fusion
  1.5 0.8 fusion.34
  2.2 0.7 copy_bitcast_fusion
  2.9 1.1 fusion.13
  4.0 0.0 copy-start.1
  4.1 1.4 %fusion.11 = (f32[64,256]{1,0:T(8,128)S(1)}, f32[64,256]{1,0:T(8,128)S(1)}) fusion(f32[1,12,64,256]{3,2,1,0:T(8,128)} %param.18, f32[64,256]{1,0:T(8,128)S(1)} %get-tuple-element.14, f32[12,64]{1,0:T(8,128)S(1)} %get-tuple-element.24, f32[12,64]{1,0:T(8,128)S(1)} %get-tuple-element.25, f32[64,256]{1,0:T(8,128)S(1)} %get-tuple-element.15), kind=kLoop, calls=%fused_computation.17 | loop fusion | flops 1540096 | bytes 1054720 | tf_op jit(solution)/shard_map/reduce_sum | solution.py:62
  5.5 1.4 %fusion.20 = (bf16[64,256]{1,0:T(8,128)(2,1)S(1)}, bf16[64,256]{1,0:T(8,128)(2,1)}) fusion(f32[64,256]{1,0:T(8,128)S(1)} %get-tuple-element.12, f32[256]{0:T(256)S(1)} %bitcast.64, s32[256]{0:T(256)} %bitcast.66, s32[64]{0:T(128)S(1)} %iota_add_fusion, f32[64,256]{1,0:T(8,128)S(1)} %get-tuple-element.13, f32[256]{0:T(256)S(1)} %bitcast.65), kind=kLoop, calls=%fused_computation.31 | loop fusion | flops 114688 | bytes 199936 | tf_op jit(solution)/shard_map/convert_element_type | solution.py:67
  6.9 0.0 copy-done.1
  6.9 20.0 %all_gather.6 = bf16[1024,256]{1,0:T(8,128)(2,1)S(1)} all-gather(bf16[64,256]{1,0:T(8,128)(2,1)S(1)} %get-tuple-element.18), channel_id=1, replica_groups=mesh['sub'=32,'blk'=16] {'blk'}, dimensions={0}, use_global_device_ids=true | all-gather | bytes 557056 | tf_op jit(solution)/shard_map/all_gather | solution.py:73
  26.8 0.0 copy-done
  26.9 0.0 copy-start.3
  26.9 0.0 copy-start.4
  26.9 0.0 copy-start.5
  26.9 0.8 fusion.4
  27.7 1.3 %copy.22 = f32[1024,256]{1,0:T(8,128)} copy(f32[1024,256]{0,1:T(8,128)S(1)} %fusion.4) | data formatting | bytes 2097152 | tf_op jit(solution)/shard_map/dot_general | solution.py:71
  29.0 0.0 copy-done.3
  29.0 0.6 pad_clamp_fusion.1
  29.6 0.0 copy-done.4
  29.6 0.2 convert_reduce_fusion
  29.8 0.6 fusion.30
  30.3 0.0 copy-done.5
  30.3 0.5 multiply_bitcast_fusion
  30.9 2.2 %scatter_custom_fusion = f32[192,256]{1,0:T(8,128)S(1)} fusion(s32[64]{0:T(128)} %fusion.30, f32[]{:T(128)} %constant.11.clone.1, f32[64,256]{1,0:T(8,128)S(1)} %get-tuple-element.12, f32[64]{0:T(128)} %multiply_bitcast_fusion, f32[1024,256]{1,0:T(8,128)} %copy.22, s32[1024]{0:T(1024)} %pad_clamp_fusion.1), kind=kCustom, calls=%fused_computation.26 | custom fusion | flops 32768 | bytes 1315840 | tf_op jit(solution)/shard_map/scatter | solution.py:24
  33.0 0.7 reshape.153
  33.8 21.0 %all-to-all-start = ((f32[32,6,256]{2,1,0:T(8,128)}), f32[32,6,256]{2,1,0:T(8,128)S(1)}, u32[]{:S(2)}, u32[]{:S(2)}) async-start(f32[32,6,256]{2,1,0:T(8,128)} %reshape.153), calls=%async_computation | async-start | bytes 524288 | tf_op jit(solution)/shard_map/all_to_all | solution.py:25
  54.8 19.7 %all_gather.7 = bf16[1024,256]{1,0:T(8,128)(2,1)S(1)} all-gather(bf16[64,256]{1,0:T(8,128)(2,1)} %get-tuple-element.19), channel_id=1, replica_groups=mesh['sub'=32,'blk'=16] {'blk'}, dimensions={0}, use_global_device_ids=true | all-gather | bytes 557056 | tf_op jit(solution)/shard_map/all_gather | solution.py:73
  74.5 1.8 %fusion.7 = f32[1024,256]{0,1:T(8,128)} fusion(bf16[1024,256]{1,0:T(8,128)(2,1)S(1)} %all_gather.7, bf16[1,1024,1024]{2,1,0:T(8,128)(2,1)S(1)} %copy-done), kind=kOutput, calls=%fused_computation.11 | convolution fusion | flops 536870912 | bytes 3670016 | tf_op jit(solution)/shard_map/dot_general | solution.py:71
  76.3 2.6 %copy.23 = f32[1024,256]{1,0:T(8,128)} copy(f32[1024,256]{0,1:T(8,128)} %fusion.7) | data formatting | bytes 2097152 | tf_op jit(solution)/shard_map/dot_general | solution.py:71
  78.9 2.8 %scatter_custom_fusion.1 = f32[192,256]{1,0:T(8,128)} fusion(s32[64]{0:T(128)} %fusion.30, f32[]{:T(128)} %constant.11.clone.1, f32[64,256]{1,0:T(8,128)S(1)} %get-tuple-element.13, f32[64]{0:T(128)} %multiply_bitcast_fusion, f32[1024,256]{1,0:T(8,128)} %copy.23, s32[1024]{0:T(1024)} %pad_clamp_fusion.1), kind=kCustom, calls=%fused_computation.24 | custom fusion | flops 32768 | bytes 1315840 | tf_op jit(solution)/shard_map/scatter | solution.py:24
  81.6 1.7 %reshape.155 = f32[32,6,256]{2,1,0:T(8,128)} reshape(f32[192,256]{1,0:T(8,128)} %scatter_custom_fusion.1) | data formatting | bytes 393216 | tf_op jit(solution)/shard_map/reshape | solution.py:26
  83.3 0.0 copy-start.2
  83.3 0.0 all-to-all-done
  83.3 16.0 %all-to-all-start.1 = ((f32[32,6,256]{2,1,0:T(8,128)}), f32[32,6,256]{2,1,0:T(8,128)}, u32[]{:S(2)}, u32[]{:S(2)}) async-start(f32[32,6,256]{2,1,0:T(8,128)} %reshape.155), calls=%async_computation.1 | async-start | bytes 524288 | tf_op jit(solution)/shard_map/all_to_all | solution.py:25
  99.3 2.2 %fusion.12 = bf16[1,1024,256]{1,2,0:T(8,128)(2,1)} fusion(f32[1024,256]{0,1:T(8,128)} %fusion.7, f32[1024,256]{0,1:T(8,128)S(1)} %fusion.4), kind=kLoop, calls=%fused_computation.18 | loop fusion | flops 1310720 | bytes 2621440 | tf_op jit(solution)/shard_map/broadcast_in_dim | solution.py:83
  101.5 2.0 %copy.24 = bf16[1,1024,256]{2,1,0:T(8,128)(2,1)} copy(bf16[1,1024,256]{1,2,0:T(8,128)(2,1)} %fusion.12) | data formatting | bytes 1048576
  103.6 0.6 pad_clamp_fusion
  104.2 0.0 copy-done.2
  104.2 2.3 %multiply_add_fusion = f32[1,12,64,256]{3,2,1,0:T(8,128)} fusion(f32[1,12,64,256]{3,2,1,0:T(8,128)} %param.18, f32[64,256]{1,0:T(8,128)S(1)} %copy-done.2, f32[64,256]{1,0:T(8,128)S(1)} %get-tuple-element.14, f32[12,64]{1,0:T(8,128)S(1)} %get-tuple-element.24, f32[12,64]{1,0:T(8,128)S(1)} %get-tuple-element.25), kind=kLoop, calls=%fused_computation.15 | loop fusion | flops 1179648 | bytes 1710080 | tf_op jit(solution)/shard_map/add | solution.py:61
  106.5 0.7 gather_fusion
  107.2 14.1 %all-to-all-done.1 = f32[32,6,256]{2,1,0:T(8,128)} async-done(((f32[32,6,256]{2,1,0:T(8,128)}), f32[32,6,256]{2,1,0:T(8,128)}, u32[]{:S(2)}, u32[]{:S(2)}) %all-to-all-start.1) | async-done | bytes 196640 | tf_op jit(solution)/shard_map/all_to_all | solution.py:25
  121.3 1.0 reshape.156
  122.3 0.7 gather_fusion.1
  123.0 0.8 copy.25
  (5 shorter events, 0.1 us)
Async XLA Ops:
  0.6 26.2 %copy-start = (bf16[1,1024,1024]{2,1,0:T(8,128)(2,1)S(1)}, bf16[1,1024,1024]{2,1,0:T(8,128)(2,1)}, u32[]{:S(2)}) copy-start(bf16[1,1024,1024]{2,1,0:T(8,128)(2,1)} %param.11) | copy-start | bytes 6291460
  4.0 2.8 %copy-start.1 = (f32[64,256]{1,0:T(8,128)}, f32[64,256]{1,0:T(8,128)S(1)}, u32[]{:S(2)}) copy-start(f32[64,256]{1,0:T(8,128)S(1)} %get-tuple-element.15) | copy-start | bytes 196612
  26.9 2.1 %copy-start.3 = (s32[1,64]{1,0:T(1,128)S(1)}, s32[1,64]{1,0:T(1,128)}, u32[]{:S(2)}) copy-start(s32[1,64]{1,0:T(1,128)} %param.12) | copy-start | bytes 772
  26.9 2.7 %copy-start.4 = (s32[1,64]{1,0:T(1,128)S(1)}, s32[1,64]{1,0:T(1,128)}, u32[]{:S(2)}) copy-start(s32[1,64]{1,0:T(1,128)} %param.13) | copy-start | bytes 772
  26.9 3.5 %copy-start.5 = (f32[1,64]{1,0:T(1,128)S(1)}, f32[1,64]{1,0:T(1,128)}, u32[]{:S(2)}) copy-start(f32[1,64]{1,0:T(1,128)} %param.15) | copy-start | bytes 772
  33.8 49.5 %all-to-all-start = ((f32[32,6,256]{2,1,0:T(8,128)}), f32[32,6,256]{2,1,0:T(8,128)S(1)}, u32[]{:S(2)}, u32[]{:S(2)}) async-start(f32[32,6,256]{2,1,0:T(8,128)} %reshape.153), calls=%async_computation | async-start | bytes 524288 | tf_op jit(solution)/shard_map/all_to_all | solution.py:25
  83.3 20.9 %copy-start.2 = (f32[64,256]{1,0:T(8,128)S(1)}, f32[64,256]{1,0:T(8,128)}, u32[]{:S(2)}) copy-start(f32[64,256]{1,0:T(8,128)} %copy-done.1) | copy-start | bytes 196612
  83.3 38.0 %all-to-all-start.1 = ((f32[32,6,256]{2,1,0:T(8,128)}), f32[32,6,256]{2,1,0:T(8,128)}, u32[]{:S(2)}, u32[]{:S(2)}) async-start(f32[32,6,256]{2,1,0:T(8,128)} %reshape.155), calls=%async_computation.1 | async-start | bytes 524288 | tf_op jit(solution)/shard_map/all_to_all | solution.py:25
where the time goes:
time: 125 us; the launch traced here: 124 us
  blocking collectives  39.7 us (32%)
  starting transfers between devices  37 us (30%)
  other arithmetic  16.7 us (13%)
  waiting for transfers between devices  14.1 us (11%)
  local copies, waits for them, and re-layouts  12.9 us (10%)
  matrix products  2.53 us (2%)
    all_gather x2, blocking collectives, body(): lax.all_gather(injections[step_index], 'blk', axis=0, tiled=True)  39.7 us
    all_to_all x2, starting transfers between devices, deliver(): lax.all_to_all(outbox.reshape(systems, capacity, columns), 'sub', split_a...  37 us
    all_to_all x2, waiting for transfers between devices, deliver(): lax.all_to_all(outbox.reshape(systems, capacity, columns), 'sub', split_a...  14.1 us
    scatter x2, other arithmetic, deliver(): jnp.zeros((systems * capacity, columns), jnp.float32).at[slot_rows]  4.93 us
    dot_general x2, local copies, waits for them, and re-layouts, body(): jnp.dot(matrix, lax.all_gather(injections[step_index], 'blk', axis=0, til...  3.92 us
    unnamed x15, local copies, waits for them, and re-layouts  3.55 us
    dot_general x2, matrix products, body(): jnp.dot(matrix, lax.all_gather(injections[step_index], 'blk', axis=0, til...  2.53 us
  transfers between devices with their start and end apart: 2, of which 1 were waited for; matrix products, arithmetic and copies ran while one was open for 13% of the time, Pallas kernels for 0%

commit v1 on v0

v1 whole, which is shorter than its diff:
```python
import functools

import jax
import jax.numpy as jnp
from jax import lax
from jax.experimental import pallas as pl
from jax.experimental.pallas import tpu as pltpu
from jax.sharding import PartitionSpec as P

MESH = pl.DeviceIdType.MESH
F32, BF16, I32 = jnp.float32, jnp.bfloat16, jnp.int32

SUBS, SIDE, PB, COLS, POLES, DEPTH, STEPS = 32, 4, 64, 256, 12, 4, 2
CAP = 6
SLOT = CAP * STEPS * 2


def kernel(
    z_hbm, port_hbm, far_hbm, delay_hbm, adm_hbm, rate_hbm, res_hbm, state_hbm, hist_hbm, event_hbm, amp_hbm,
    peak_hbm, new_hbm, arr_hbm,
    z_v, port_v, far_v, delay_v, adm_v, rate_v, res_v, state_v, hist_v, event_v, amp_v,
    peak_ref, new_ref, arr_ref, table, gath, source, ports, outbox, inbox,
    in_sem, done_sem, s1, r1, s2, r2, s3, r3, s4, r4, out_sem, box_sem,
):
    sub = lax.axis_index("sub")
    blk = lax.axis_index("blk")
    x = lax.rem(blk, SIDE)
    y = lax.div(blk, SIDE)
    xs = (lax.rem(x + 3, SIDE), lax.rem(x + 1, SIDE))
    ys = (lax.rem(y + 3, SIDE), lax.rem(y + 1, SIDE))
    by_x = tuple(y * SIDE + v for v in xs)
    by_y = tuple(v * SIDE + x for v in ys)

    loads = {}
    pairs = (
        (port_hbm, port_v), (far_hbm, far_v), (delay_hbm, delay_v), (adm_hbm, adm_v), (rate_hbm, rate_v),
        (res_hbm, res_v), (event_hbm, event_v), (amp_hbm, amp_v), (hist_hbm, hist_v), (state_hbm, state_v), (z_hbm, z_v),
    )
    for n, (src, dst) in enumerate(pairs):
        loads[n] = pltpu.make_async_copy(src, dst, in_sem.at[n])
        loads[n].start()

    barrier = pltpu.get_barrier_semaphore()
    for b in by_x + by_y:
        pl.semaphore_signal(barrier, inc=1, device_id=(sub, b), device_id_type=MESH)

    def greet(k, c):
        pl.semaphore_signal(barrier, inc=1, device_id=(lax.rem(sub + k, SUBS), blk), device_id_type=MESH)
        return c

    lax.fori_loop(1, SUBS, greet, 0)

    for n in range(8):
        loads[n].wait()
    table[...] = jnp.zeros_like(table)
    table[0:POLES, 0:PB] = rate_v[:, 0, :]
    table[16:16 + POLES, 0:PB] = res_v[:, 0, :]
    table[32:33, 0:PB] = adm_v[...]
    table[33:34, 0:PB] = far_v[...].astype(F32)
    table[34:35, 0:PB] = (port_v[...] - blk * 1024).astype(F32)
    table[35:36, 0:PB] = delay_v[...].astype(F32)
    turned = jnp.transpose(table[...])

    loads[8].wait()
    loads[9].wait()
    for part in range(4):
        rows = slice(part * 16, part * 16 + 16)
        delay = turned[rows, 35:36]
        arrive = []
        for step in range(STEPS):
            got = jnp.zeros((16, COLS), F32)
            for d in range(DEPTH):
                got = jnp.where(delay == float(d + step + 1), hist_v[0, d, rows, :], got)
            arrive.append(got)
        totals = [jnp.zeros((16, COLS), F32) for _ in range(STEPS)]
        for p in range(POLES):
            rate = turned[rows, p:p + 1]
            weight = turned[rows, 16 + p:17 + p]
            now = state_v[0, p, rows, :]
            for step in range(STEPS):
                now = rate * now + weight * arrive[step]
                totals[step] = totals[step] + now
            new_ref[0, p, rows, :] = now
        index = lax.broadcasted_iota(I32, (16, COLS), 0) + (blk * PB + part * 16)
        hit = event_v[...] == index
        for step in range(STEPS):
            source[step, rows, :] = totals[step]
            kick = jnp.where(hit, amp_v[0, step:step + 1, :], 0.0)
            gath[step, y, pl.ds(pl.multiple_of(x * PB + part * 16, 16), 16), :] = (totals[step] + kick).astype(BF16)

    stores = [pltpu.make_async_copy(new_ref, new_hbm, done_sem.at[0])]
    stores[0].start()
    pl.semaphore_wait(barrier, 4 + SUBS - 1)

    def send(src, peer, s, r):
        c = pltpu.make_async_remote_copy(
            src_ref=src, dst_ref=src, send_sem=s, recv_sem=r, device_id=(sub, peer), device_id_type=MESH)
        c.start()
        return c

    def slab(step, yy, xx, lo, n):
        return gath.at[step, yy, pl.ds(pl.multiple_of(xx * PB + lo, 16), n), :]

    near = (by_x, by_y)
    far = (by_y, by_x)
    c1 = [[send(slab(t, y, x, 0, PB), near[t][1 - w], s1.at[t, w], r1.at[t, w]) for w in range(2)] for t in range(2)]

    far_row = far_v[...].astype(F32)
    far_col = turned[0:PB, 33:34]
    node_col = turned[0:PB, 34:35]
    same = far_col == far_row
    ii = lax.broadcasted_iota(I32, (PB, PB), 0)
    jj = lax.broadcasted_iota(I32, (PB, PB), 1)
    rank_row = jnp.sum(jnp.where(same & (ii < jj), 1.0, 0.0), axis=0, keepdims=True)
    rank_col = jnp.sum(jnp.where(same & (jj < ii), 1.0, 0.0), axis=1, keepdims=True)
    slot_row = (far_row * SLOT + rank_row).astype(I32)
    slot_col = (far_col * SLOT + rank_col).astype(I32)
    place_row = jnp.concatenate([slot_row + q * CAP for q in range(4)], axis=1)
    place_col = jnp.concatenate([slot_col + q * CAP for q in range(4)], axis=0)
    pick = (lax.broadcasted_iota(I32, (PB, 1024), 1) == node_col.astype(I32)).astype(BF16)

    c2 = [[None, None], [None, None]]
    for t in range(2):
        for w in range(2):
            c1[t][w].wait_recv()
            yy, xx = (y, xs[w]) if t == 0 else (ys[w], x)
            c2[t][w] = send(slab(t, yy, xx, 32 * w, 32), near[t][1 - w], s2.at[t, w], r2.at[t, w])

    loads[10].wait()
    ports[...] = jnp.dot(pick, z_v[0], preferred_element_type=F32).astype(BF16)

    c3 = [[None, None], [None, None]]
    for t in range(2):
        for w in range(2):
            c2[t][w].wait_recv()
        line = gath.at[0, y] if t == 0 else gath.at[1, :, pl.ds(pl.multiple_of(x * PB, 16), PB), :]
        for w in range(2):
            c3[t][w] = send(line, far[t][1 - w], s3.at[t, w], r3.at[t, w])
    c4 = [[None, None], [None, None]]
    for t in range(2):
        for w in range(2):
            c3[t][w].wait_recv()
            if t == 0:
                half = gath.at[0, ys[w], pl.ds(128 * w, 128), :]
            else:
                half = gath.at[1, pl.ds(2 * w, 2), pl.ds(pl.multiple_of(xs[w] * PB, 16), PB), :]
            c4[t][w] = send(half, far[t][1 - w], s4.at[t, w], r4.at[t, w])
    for t in range(2):
        for w in range(2):
            c4[t][w].wait_recv()

    twice = 2.0 * turned[0:PB, 32:33]
    waves = []
    for t in range(2):
        volt = jnp.dot(ports[...], gath[t].reshape(1024, COLS), preferred_element_type=F32)
        wave = (twice * volt - source[t]).astype(BF16)
        waves += [wave[:, 0:128], wave[:, 128:256]]
    stacked = jnp.concatenate(waves, axis=0)
    pack = (lax.broadcasted_iota(I32, (SUBS * SLOT, 256), 0) == place_row).astype(BF16)
    boxes = jnp.dot(pack, stacked, preferred_element_type=F32).astype(BF16)
    outbox[...] = boxes.reshape(SUBS, SLOT, 128)

    def box(k):
        d = lax.rem(sub + k, SUBS)
        return pltpu.make_async_remote_copy(
            src_ref=outbox.at[d], dst_ref=inbox.at[sub], send_sem=out_sem.at[d], recv_sem=box_sem.at[sub],
            device_id=(d, blk), device_id_type=MESH)

    box(16).start()

    def post(i, c):
        box(15 - i).start()
        box(17 + i).start()
        return c

    lax.fori_loop(0, 15, post, 0)
    inbox[sub] = jnp.zeros((SLOT, 128), BF16)

    for part in range(4):
        rows = slice(part * 256, part * 256 + 256)
        v0 = jnp.dot(z_v[0, rows, :], gath[0].reshape(1024, COLS), preferred_element_type=F32)
        v1 = jnp.dot(z_v[0, rows, :], gath[1].reshape(1024, COLS), preferred_element_type=F32)
        peak_ref[0, rows, :] = jnp.maximum(jnp.abs(v0), jnp.abs(v1)).astype(BF16)

    stores.append(pltpu.make_async_copy(peak_ref, peak_hbm, done_sem.at[1]))
    stores[1].start()
    unpack = (lax.broadcasted_iota(I32, (256, SUBS * SLOT), 1) == place_col).astype(BF16)

    def collect(k, c):
        d = lax.rem(sub + k, SUBS)
        pltpu.make_async_remote_copy(
            src_ref=outbox.at[d], dst_ref=inbox.at[d], send_sem=out_sem.at[d], recv_sem=box_sem.at[d],
            device_id=(d, blk), device_id_type=MESH).wait_recv()
        return c

    lax.fori_loop(1, SUBS, collect, 0)
    got = jnp.dot(unpack, inbox[...].reshape(SUBS * SLOT, 128), preferred_element_type=F32)
    for t in range(2):
        arr_ref[0, :, t, 0:128] = got[128 * t:128 * t + PB]
        arr_ref[0, :, t, 128:256] = got[128 * t + PB:128 * t + 2 * PB]
    stores.append(pltpu.make_async_copy(arr_ref, arr_hbm, done_sem.at[2]))
    stores[2].start()

    for t in range(2):
        for w in range(2):
            for c in (c1, c2, c3, c4):
                c[t][w].wait_send()

    def drain(k, c):
        box(k).wait_send()
        return c

    lax.fori_loop(1, SUBS, drain, 0)
    for c in stores:
        c.wait()


def body(*args):
    args = list(args)
    for n in (5, 6):
        args[n] = args[n].reshape(POLES, 1, PB)
    dma = pltpu.SemaphoreType.DMA
    outs = (
        jax.ShapeDtypeStruct((1, 1024, COLS), BF16),
        jax.ShapeDtypeStruct((1, POLES, PB, COLS), F32),
        jax.ShapeDtypeStruct((1, PB, STEPS, COLS), F32),
    )
    return pl.pallas_call(
        kernel,
        out_shape=outs,
        in_specs=[pl.BlockSpec(memory_space=pltpu.HBM)] * len(args),
        out_specs=[pl.BlockSpec(memory_space=pltpu.HBM)] * 3,
        scratch_shapes=[pltpu.VMEM(a.shape, a.dtype) for a in (*args, *outs)] + [
            pltpu.VMEM((128, 128), F32),
            pltpu.VMEM((2, SIDE, SIDE * PB, COLS), BF16),
            pltpu.VMEM((2, PB, COLS), F32),
            pltpu.VMEM((PB, 1024), BF16),
            pltpu.VMEM((SUBS, SLOT, 128), BF16),
            pltpu.VMEM((SUBS, SLOT, 128), BF16),
            dma((len(args),)),
            dma((3,)),
        ] + [dma((2, 2))] * 8 + [dma((SUBS,))] * 2,
        compiler_params=pltpu.CompilerParams(
            collective_id=0, has_side_effects=True, vmem_limit_bytes=60 * 1024 * 1024),
    )(*args)


def solution(mesh):
    placed = (
        P("sub", "blk", None),
        P("sub", "blk"),
        P("sub", "blk"),
        P("sub", "blk"),
        P("sub", "blk"),
        P("sub", None, "blk"),
        P("sub", None, "blk"),
        P("sub", None, "blk", None),
        P("sub", None, "blk", None),
        P("sub", None),
        P("sub", None, None),
    )
    return jax.shard_map(
        body,
        mesh=mesh,
        in_specs=placed,
        out_specs=(P("sub", "blk", None), P("sub", None, "blk", None), P("sub", "blk", None, None)),
        check_vma=False,
    )
```

time: 125 us -> 49.6 us (0.40)
  Pallas kernels: 0 us -> 44.1 us
  blocking collectives: 39.7 us -> 0 us
  starting transfers between devices: 37 us -> 0 us
  other arithmetic: 16.7 us -> 0 us
  waiting for transfers between devices: 14.1 us -> 0 us
  local copies, waits for them, and re-layouts: 12.9 us -> 4.63 us
  matrix products: 2.53 us -> 0 us
    pallas_call x0 -> x1, Pallas kernels: none -> 44.1 us  [body(): pl.pallas_call(kernel, out_shape=outs, in_specs=[pl.BlockSpec(memory_spac...]
    all_gather x2 -> x0, blocking collectives: 39.7 us -> none  [body(): lax.all_gather(injections[step_index], 'blk', axis=0, tiled=True)]
    all_to_all x2 -> x0, starting transfers between devices: 37 us -> none  [deliver(): lax.all_to_all(outbox.reshape(systems, capacity, columns), 'sub', split_a...]
    all_to_all x2 -> x0, waiting for transfers between devices: 14.1 us -> none  [deliver(): lax.all_to_all(outbox.reshape(systems, capacity, columns), 'sub', split_a...]
    scatter x2 -> x0, other arithmetic: 4.93 us -> none  [deliver(): jnp.zeros((systems * capacity, columns), jnp.float32).at[slot_rows]]
    dot_general x2 -> x0, local copies, waits for them, and re-layouts: 3.92 us -> none  [body(): jnp.dot(matrix, lax.all_gather(injections[step_index], 'blk', axis=0, til...]
    reshape x4 -> x0, local copies, waits for them, and re-layouts: 3.4 us -> none  [the longest x2 2.4 us: deliver(): outbox.reshape(systems, capacity, columns)]
    reduce_sum x3 -> x0, other arithmetic: 2.71 us -> none  [the longest x1 1.44 us: body(): source = jnp.sum(current, axis=0)]
  transfers between devices with their start and end apart: 2 -> 0, of which waited for: 1 -> 0; matrix products, arithmetic and copies ran while one was open for 13% -> 0% of each run, Pallas kernels for 0% -> 0%
where the time goes in v1:
time: 49.6 us; the launch traced here: 49.4 us
  Pallas kernels  44.1 us (89%)
  local copies, waits for them, and re-layouts  4.63 us (9%)
  between operations  0.65 us (1%)
    pallas_call x1, Pallas kernels, body(): pl.pallas_call(kernel, out_shape=outs, in_specs=[pl.BlockSpec(memory_spac...  44.1 us
    unnamed x5, local copies, waits for them, and re-layouts  4.63 us

profile of v1, /device:TPU:1, one launch (start us, length us, event | category | flops | bytes accessed | tf_op | source)
XLA Modules:
  0.0 49.4 jit_solution(10392752787151318449)
XLA Ops:
  0.6 44.1 %shard_map.130 = (bf16[1,1024,256]{2,1,0:T(8,128)(2,1)}, f32[1,12,64,256]{3,2,1,0:T(8,128)}, f32[1,64,2,256]{3,2,1,0:T(2,128)}) custom-call(bf16[1,1024,1024]{2,1,0:T(8,128)(2,1)} %z_hbm.1, s32[1,64]{1,0:T(1,128)} %port_hbm.1, s32[1,64]{1,0:T(1,128)} %far_hbm.1, s32[1,64]{1,0:T(1,128)} %delay_hbm.1, f32[1,64]{1,0:T(1,128)} %adm_hbm.1, f32[12,1,64]{2,1,0:T(1,128)} %bitcast.2, ...), custom_call_target="tpu_custom_call" | custom-call | tf_op jit(solution)/shard_map/pallas_call | solution.py:228
  44.7 0.0 copy-start
  44.8 1.9 %copy.17 = bf16[1,1024,256]{2,1,0:T(8,128)(2,1)} copy(bf16[1,1024,256]{2,1,0:T(8,128)(2,1)} %get-tuple-element.6) | data formatting | bytes 1048576
  46.7 2.1 %copy.18 = f32[1,12,64,256]{3,2,1,0:T(8,128)} copy(f32[1,12,64,256]{3,2,1,0:T(8,128)} %get-tuple-element.7) | data formatting | bytes 1572864
  48.7 0.0 copy-done
  48.7 0.7 %copy.19 = f32[1,64,2,256]{3,2,1,0:T(2,128)} copy(f32[1,64,2,256]{3,2,1,0:T(2,128)S(1)} %copy-done) | data formatting | bytes 262144
Async XLA Ops:
  44.7 4.0 %copy-start = (f32[1,64,2,256]{3,2,1,0:T(2,128)S(1)}, f32[1,64,2,256]{3,2,1,0:T(2,128)}, u32[]{:S(2)}) copy-start(f32[1,64,2,256]{3,2,1,0:T(2,128)} %get-tuple-element.8) | copy-start | bytes 393220

commit v2 on v1

v2 whole, which is shorter than its diff:
```python
import jax
import jax.numpy as jnp
from jax import lax
from jax.experimental import pallas as pl
from jax.experimental.pallas import tpu as pltpu
from jax.sharding import PartitionSpec as P

MESH = pl.DeviceIdType.MESH
F32, BF16, I32 = jnp.float32, jnp.bfloat16, jnp.int32

SUBS, SIDE, PB, NB, COLS, POLES, DEPTH, STEPS = 32, 4, 64, 1024, 256, 12, 4, 2
CAP = 6
SLOT = CAP * STEPS * 2
HOPS = (1, 3, 2)
NEAR = (1,) + tuple(2 * k + c for k in (1, 15, 2, 14, 3, 13, 4, 12) for c in range(2))


def turn_tables(blk, small, table):
    port_v, far_v, delay_v, adm_v, rate_v, res_v = small
    table[...] = jnp.zeros_like(table)
    table[0:POLES, 0:PB] = rate_v[:, 0, :]
    table[16:16 + POLES, 0:PB] = res_v[:, 0, :]
    table[32:33, 0:PB] = adm_v[...]
    table[33:34, 0:PB] = far_v[...].astype(F32)
    table[34:35, 0:PB] = (port_v[...] - blk * NB).astype(F32)
    table[35:36, 0:PB] = delay_v[...].astype(F32)
    table[...] = jnp.transpose(table[...])


def advance(x, y, table, state_v, hist_v, event_v, amp_v, new_v, source, gath):
    for part in range(4):
        rows = slice(part * 16, part * 16 + 16)
        delay = table[rows, 35:36]
        arrive = []
        for step in range(STEPS):
            got = jnp.zeros((16, COLS), F32)
            for d in range(DEPTH):
                got = jnp.where(delay == float(d + step + 1), hist_v[0, d, rows, :], got)
            arrive.append(got)
        totals = [jnp.zeros((16, COLS), F32) for _ in range(STEPS)]
        for p in range(POLES):
            rate = table[rows, p:p + 1]
            weight = table[rows, 16 + p:17 + p]
            now = state_v[0, p, rows, :]
            for step in range(STEPS):
                now = rate * now + weight * arrive[step]
                totals[step] = totals[step] + now
            new_v[0, p, rows, :] = now
        index = lax.broadcasted_iota(I32, (16, COLS), 0) + ((y * SIDE + x) * PB + part * 16)
        hit = event_v[...] == index
        for step in range(STEPS):
            source[step, rows, :] = totals[step]
            kick = jnp.where(hit, amp_v[0, step:step + 1, :], 0.0)
            gath[step, y, pl.ds(pl.multiple_of(x * PB + part * 16, 16), 16), :] = (totals[step] + kick).astype(BF16)


def places(far_v, table):
    far_row = far_v[...].astype(F32)
    far_col = table[0:PB, 33:34]
    same = far_col == far_row
    ii = lax.broadcasted_iota(I32, (PB, PB), 0)
    jj = lax.broadcasted_iota(I32, (PB, PB), 1)
    rank_row = jnp.sum(jnp.where(same & (ii < jj), 1.0, 0.0), axis=0, keepdims=True)
    rank_col = jnp.sum(jnp.where(same & (jj < ii), 1.0, 0.0), axis=1, keepdims=True)
    slot_row = (far_row * SLOT + rank_row).astype(I32)
    slot_col = (far_col * SLOT + rank_col).astype(I32)
    place_row = jnp.concatenate([slot_row + q * CAP for q in range(4)], axis=1)
    place_col = jnp.concatenate([slot_col + q * CAP for q in range(4)], axis=0)
    return place_row, place_col


def masks(far_v, table, pack, unpack):
    place_row, place_col = places(far_v, table)
    pack[...] = (lax.broadcasted_iota(I32, (SUBS * SLOT, 256), 0) == place_row).astype(BF16)
    unpack[...] = (lax.broadcasted_iota(I32, (256, SUBS * SLOT), 1) == place_col).astype(BF16)


def port_rows(table, z_v, ports):
    node_col = table[0:PB, 34:35].astype(I32)
    pick = (lax.broadcasted_iota(I32, (PB, NB), 1) == node_col).astype(BF16)
    ports[...] = jnp.dot(pick, z_v[0], preferred_element_type=F32).astype(BF16)


def waves_out(table, ports, gath, source, pack, outbox):
    twice = 2.0 * table[0:PB, 32:33]
    waves = []
    for t in range(2):
        volt = jnp.dot(ports[...], gath[t].reshape(1024, COLS), preferred_element_type=F32)
        wave = (twice * volt - source[t]).astype(BF16)
        waves += [wave[:, 0:128], wave[:, 128:256]]
    stacked = jnp.concatenate(waves, axis=0)
    boxes = jnp.dot(pack[...], stacked, preferred_element_type=F32).astype(BF16)
    outbox[...] = boxes.reshape(SUBS, SLOT, 128)


def peaks(z_v, gath, peak_ref):
    for part in range(4):
        rows = slice(part * 256, part * 256 + 256)
        v0 = jnp.dot(z_v[0, rows, :], gath[0].reshape(1024, COLS), preferred_element_type=F32)
        v1 = jnp.dot(z_v[0, rows, :], gath[1].reshape(1024, COLS), preferred_element_type=F32)
        peak_ref[0, rows, :] = jnp.maximum(jnp.abs(v0), jnp.abs(v1)).astype(BF16)


def spread(unpack, inbox, arr_ref):
    got = jnp.dot(unpack[...], inbox[...].reshape(SUBS * SLOT, 128), preferred_element_type=F32)
    for t in range(2):
        arr_ref[0, :, t, 0:128] = got[128 * t:128 * t + PB]
        arr_ref[0, :, t, 128:256] = got[128 * t + PB:128 * t + 2 * PB]


def kernel(
    z_hbm, port_hbm, far_hbm, delay_hbm, adm_hbm, rate_hbm, res_hbm, state_hbm, hist_hbm, event_hbm, amp_hbm,
    peak_ref, new_ref, inbox, unpack,
    z_v, port_v, far_v, delay_v, adm_v, rate_v, res_v, state_v, hist_v, event_v, amp_v,
    table, gath, source, ports, outbox, pack,
    in_sem, ring_s, ring_r, out_sem, box_sem, met,
):
    sub = lax.axis_index("sub")
    blk = lax.axis_index("blk")
    x = lax.rem(blk, SIDE)
    y = lax.div(blk, SIDE)

    loads = []
    pairs = (
        (port_hbm, port_v), (far_hbm, far_v), (delay_hbm, delay_v), (adm_hbm, adm_v), (rate_hbm, rate_v),
        (res_hbm, res_v), (event_hbm, event_v), (amp_hbm, amp_v), (hist_hbm, hist_v), (state_hbm, state_v), (z_hbm, z_v),
    )
    for n, (src, dst) in enumerate(pairs):
        loads.append(pltpu.make_async_copy(src, dst, in_sem.at[n]))
        loads[n].start()

    def along(axis, k):
        if axis == 0:
            return y, lax.rem(x + k, SIDE)
        return lax.rem(y + k, SIDE), x

    barrier = pltpu.get_barrier_semaphore()
    for axis in range(2):
        for k in HOPS:
            py, px = along(axis, k)
            pl.semaphore_signal(barrier, inc=1, device_id=(sub, py * SIDE + px), device_id_type=MESH)

    def near(sem):
        for k in NEAR:
            z = lax.rem(lax.div(sub, 2) + k // 2, SUBS // 2)
            core = lax.rem(lax.rem(sub, 2) + k, 2)
            pl.semaphore_signal(sem, inc=1, device_id=(z * 2 + core, blk), device_id_type=MESH)

    near(barrier)

    for n in range(8):
        loads[n].wait()
    turn_tables(blk, (port_v, far_v, delay_v, adm_v, rate_v, res_v), table)
    loads[8].wait()
    loads[9].wait()
    advance(x, y, table, state_v, hist_v, event_v, amp_v, new_ref, source, gath)

    pl.semaphore_wait(barrier, 6 + len(NEAR))

    def slab(t, yy, xx, axis, k, level):
        ref = gath.at[t, yy, pl.ds(pl.multiple_of(xx * PB, 16), PB), :]
        py, px = along(axis, k)
        c = pltpu.make_async_remote_copy(
            src_ref=ref, dst_ref=ref, send_sem=ring_s.at[level, t, k], recv_sem=ring_r.at[level, t, k],
            device_id=(sub, py * SIDE + px), device_id_type=MESH)
        c.start()
        return c

    first = [[slab(t, y, x, t, k, 0) for k in HOPS] for t in range(2)]
    later = [slab(t, y, x, 1 - t, k, 1) for t in range(2) for k in HOPS]

    near(met)
    masks(far_v, table, pack, unpack)
    for n, k in enumerate(HOPS):
        for t in range(2):
            first[t][n].wait_recv()
            yy, xx = along(t, SIDE - k)
            later += [slab(t, yy, xx, 1 - t, j, 1 + k) for j in HOPS]
        if n == 0:
            loads[10].wait()
            port_rows(table, z_v, ports)
    for c in later:
        c.wait_recv()

    waves_out(table, ports, gath, source, pack, outbox)
    pl.semaphore_wait(met, len(NEAR))

    def box(k):
        d = lax.rem(sub + k, SUBS)
        return pltpu.make_async_remote_copy(
            src_ref=outbox.at[d], dst_ref=inbox.at[sub], send_sem=out_sem.at[d], recv_sem=box_sem.at[sub],
            device_id=(d, blk), device_id_type=MESH)

    def post(i, c):
        box(lax.rem(i + SUBS - sub, SUBS)).start()
        return c

    lax.fori_loop(0, sub, post, 0)
    lax.fori_loop(sub + 1, SUBS, post, 0)
    inbox[sub] = jnp.zeros((SLOT, 128), BF16)
    peaks(z_v, gath, peak_ref)

    def collect(k, c):
        d = lax.rem(sub + k, SUBS)
        pltpu.make_async_remote_copy(
            src_ref=outbox.at[d], dst_ref=inbox.at[d], send_sem=out_sem.at[d], recv_sem=box_sem.at[d],
            device_id=(d, blk), device_id_type=MESH).wait_recv()
        return c

    lax.fori_loop(1, SUBS, collect, 0)

    for c in first[0] + first[1] + later:
        c.wait_send()

    def drain(k, c):
        box(k).wait_send()
        return c

    lax.fori_loop(1, SUBS, drain, 0)


def settle(peak, new, inbox, unpack, peak_hbm, new_hbm, arr_hbm, arr, sem):
    copies = [pltpu.make_async_copy(a, b, sem.at[n]) for n, (a, b) in enumerate(((peak, peak_hbm), (new, new_hbm), (arr, arr_hbm)))]
    copies[0].start()
    copies[1].start()
    spread(unpack, inbox, arr)
    copies[2].start()
    for q in copies:
        q.wait()


HELD = (
    ((1, NB, COLS), BF16), ((1, POLES, PB, COLS), F32), ((SUBS, SLOT, 128), BF16), ((256, SUBS * SLOT), BF16),
)
OUTS = (((1, NB, COLS), BF16), ((1, POLES, PB, COLS), F32), ((1, PB, STEPS, COLS), F32))


def scratch(args):
    dma = pltpu.SemaphoreType.DMA
    return [pltpu.VMEM(a.shape, a.dtype) for a in args] + [
        pltpu.VMEM((128, 128), F32),
        pltpu.VMEM((2, SIDE, SIDE * PB, COLS), BF16),
        pltpu.VMEM((2, PB, COLS), F32),
        pltpu.VMEM((PB, 1024), BF16),
        pltpu.VMEM((SUBS, SLOT, 128), BF16),
        pltpu.VMEM((SUBS * SLOT, 256), BF16),
        dma((len(args),)),
        dma((5, 2, 4)),
        dma((5, 2, 4)),
        dma((SUBS,)),
        dma((SUBS,)),
        pltpu.SemaphoreType.REGULAR,
    ]


def body(*args):
    args = list(args)
    for n in (5, 6):
        args[n] = args[n].reshape(POLES, 1, PB)
    args = [pltpu.with_memory_space_constraint(a, pltpu.HBM) for a in args]
    held = pl.pallas_call(
        kernel,
        out_shape=[pltpu.VMEM(s, d) for s, d in HELD],
        in_specs=[pl.BlockSpec(memory_space=pltpu.HBM)] * len(args),
        out_specs=[pl.BlockSpec(memory_space=pltpu.VMEM)] * 4,
        scratch_shapes=scratch(args),
        compiler_params=pltpu.CompilerParams(
            collective_id=0, has_side_effects=True, vmem_limit_bytes=32 * 1024 * 1024),
    )(*args)
    held = [pltpu.with_memory_space_constraint(a, pltpu.VMEM) for a in held]
    return pl.pallas_call(
        settle,
        out_shape=[pltpu.HBM(s, d) for s, d in OUTS],
        in_specs=[pl.BlockSpec(memory_space=pltpu.VMEM)] * 4,
        out_specs=[pl.BlockSpec(memory_space=pltpu.HBM)] * 3,
        scratch_shapes=[pltpu.VMEM(*OUTS[2]), pltpu.SemaphoreType.DMA((3,))],
    )(*held)


def solution(mesh):
    placed = (
        P("sub", "blk", None),
        P("sub", "blk"),
        P("sub", "blk"),
        P("sub", "blk"),
        P("sub", "blk"),
        P("sub", None, "blk"),
        P("sub", None, "blk"),
        P("sub", None, "blk", None),
        P("sub", None, "blk", None),
        P("sub", None),
        P("sub", None, None),
    )
    return jax.shard_map(
        body,
        mesh=mesh,
        in_specs=placed,
        out_specs=(P("sub", "blk", None), P("sub", None, "blk", None), P("sub", "blk", None, None)),
        check_vma=False,
    )
```

time: 49.6 us -> 37.4 us (0.75)
  Pallas kernels: 44.1 us -> 36.6 us
  local copies, waits for them, and re-layouts: 4.63 us -> 0 us
    pallas_call x1 -> x2, Pallas kernels: 44.1 us -> 36.6 us  [the longest x1 35.5 us: body(): pl.pallas_call(kernel, out_shape=[pltpu.VMEM(s, d) for s, d in HELD], in_...]
    unnamed x5 -> x0, local copies, waits for them, and re-layouts: 4.63 us -> none
where the time goes in v2:
time: 37.4 us; the launch traced here: 37.2 us
  Pallas kernels  36.6 us (98%)
  between operations  0.64 us (2%)
    pallas_call x1, Pallas kernels, body(): pl.pallas_call(kernel, out_shape=[pltpu.VMEM(s, d) for s, d in HELD], in_...  35.5 us
    pallas_call x1, Pallas kernels, body(): pl.pallas_call(settle, out_shape=[pltpu.HBM(s, d) for s, d in OUTS], in_s...  1.12 us

profile of v2, /device:TPU:1, one launch (start us, length us, event | category | flops | bytes accessed | tf_op | source)
XLA Modules:
  0.0 37.2 jit_solution(1673861904401977831)
XLA Ops:
  0.6 35.5 %shard_map.130 = (bf16[1,1024,256]{2,1,0:T(8,128)(2,1)S(1)}, f32[1,12,64,256]{3,2,1,0:T(8,128)S(1)}, bf16[32,24,128]{2,1,0:T(8,128)(2,1)S(1)}, bf16[256,768]{1,0:T(8,128)(2,1)S(1)}) custom-call(bf16[1,1024,1024]{2,1,0:T(8,128)(2,1)} %z_hbm.1, s32[1,64]{1,0:T(1,128)} %port_hbm.1, s32[1,64]{1,0:T(1,128)} %far_hbm.1, s32[1,64]{1,0:T(1,128)} %delay_hbm.1, ...), custom_call_target="tpu_custom_call" | custom-call | tf_op jit(solution)/shard_map/pallas_call | solution.py:261
  36.1 1.1 %shard_map.131 = (bf16[1,1024,256]{2,1,0:T(8,128)(2,1)}, f32[1,12,64,256]{3,2,1,0:T(8,128)}, f32[1,64,2,256]{3,2,1,0:T(2,128)}) custom-call(bf16[1,1024,256]{2,1,0:T(8,128)(2,1)S(1)} %get-tuple-element.7.peak, f32[1,12,64,256]{3,2,1,0:T(8,128)S(1)} %get-tuple-element.8.new, bf16[32,24,128]{2,1,0:T(8,128)(2,1)S(1)} %get-tuple-element.9.inbox, ...), custom_call_target="tpu_custom_call" | custom-call | tf_op jit(solution)/shard_map/pallas_call | solution.py:271

commit v3 on v2

--- a/solution.py
+++ b/solution.py
@@ -12,7 +12,8 @@
 CAP = 6
 SLOT = CAP * STEPS * 2
 HOPS = (1, 3, 2)
-NEAR = (1,) + tuple(2 * k + c for k in (1, 15, 2, 14, 3, 13, 4, 12) for c in range(2))
+NEAR = ((0, 1),) + tuple((k, c) for k in (1, 15, 2, 14) for c in range(2))
+WIDE = ((4, 0), (12, 0))
 
 
 def turn_tables(blk, small, table):
@@ -93,8 +94,8 @@
     outbox[...] = boxes.reshape(SUBS, SLOT, 128)
 
 
-def peaks(z_v, gath, peak_ref):
-    for part in range(4):
+def peaks(z_v, gath, peak_ref, part):
+    for part in (part,):
         rows = slice(part * 256, part * 256 + 256)
         v0 = jnp.dot(z_v[0, rows, :], gath[0].reshape(1024, COLS), preferred_element_type=F32)
         v1 = jnp.dot(z_v[0, rows, :], gath[1].reshape(1024, COLS), preferred_element_type=F32)
@@ -113,7 +114,7 @@
     peak_ref, new_ref, inbox, unpack,
     z_v, port_v, far_v, delay_v, adm_v, rate_v, res_v, state_v, hist_v, event_v, amp_v,
     table, gath, source, ports, outbox, pack,
-    in_sem, ring_s, ring_r, out_sem, box_sem, met,
+    in_sem, ring_s, ring_r, out_sem, box_sem, met, wide,
 ):
     sub = lax.axis_index("sub")
     blk = lax.axis_index("blk")
@@ -127,7 +128,8 @@
     )
     for n, (src, dst) in enumerate(pairs):
         loads.append(pltpu.make_async_copy(src, dst, in_sem.at[n]))
-        loads[n].start()
+        if n < 10:
+            loads[n].start()
 
     def along(axis, k):
         if axis == 0:
@@ -140,19 +142,21 @@
             py, px = along(axis, k)
             pl.semaphore_signal(barrier, inc=1, device_id=(sub, py * SIDE + px), device_id_type=MESH)
 
-    def near(sem):
-        for k in NEAR:
-            z = lax.rem(lax.div(sub, 2) + k // 2, SUBS // 2)
-            core = lax.rem(lax.rem(sub, 2) + k, 2)
-            pl.semaphore_signal(sem, inc=1, device_id=(z * 2 + core, blk), device_id_type=MESH)
-
-    near(barrier)
+    chip, core = lax.div(sub, 2), lax.rem(sub, 2)
+
+    def tell(sem, offsets):
+        for k, c in offsets:
+            peer = lax.rem(chip + k, SUBS // 2) * 2 + lax.rem(core + c, 2)
+            pl.semaphore_signal(sem, inc=1, device_id=(peer, blk), device_id_type=MESH)
+
+    tell(barrier, NEAR)
 
     for n in range(8):
         loads[n].wait()
     turn_tables(blk, (port_v, far_v, delay_v, adm_v, rate_v, res_v), table)
     loads[8].wait()
     loads[9].wait()
+    loads[10].start()
     advance(x, y, table, state_v, hist_v, event_v, amp_v, new_ref, source, gath)
 
     pl.semaphore_wait(barrier, 6 + len(NEAR))
@@ -169,7 +173,7 @@
     first = [[slab(t, y, x, t, k, 0) for k in HOPS] for t in range(2)]
     later = [slab(t, y, x, 1 - t, k, 1) for t in range(2) for k in HOPS]
 
-    near(met)
+    tell(met, NEAR)
     masks(far_v, table, pack, unpack)
     for n, k in enumerate(HOPS):
         for t in range(2):
@@ -177,13 +181,15 @@
             yy, xx = along(t, SIDE - k)
             later += [slab(t, yy, xx, 1 - t, j, 1 + k) for j in HOPS]
         if n == 0:
+            pl.semaphore_wait(met, len(NEAR))
+            tell(wide, WIDE)
             loads[10].wait()
             port_rows(table, z_v, ports)
     for c in later:
         c.wait_recv()
 
     waves_out(table, ports, gath, source, pack, outbox)
-    pl.semaphore_wait(met, len(NEAR))
+    pl.semaphore_wait(wide, len(WIDE))
 
     def box(k):
         d = lax.rem(sub + k, SUBS)
@@ -195,10 +201,12 @@
         box(lax.rem(i + SUBS - sub, SUBS)).start()
         return c
 
-    lax.fori_loop(0, sub, post, 0)
-    lax.fori_loop(sub + 1, SUBS, post, 0)
+    for part in range(4):
+        lo = part * 8
+        lax.fori_loop(lo, jnp.clip(sub, lo, lo + 8), post, 0)
+        lax.fori_loop(jnp.clip(sub + 1, lo, lo + 8), lo + 8, post, 0)
+        peaks(z_v, gath, peak_ref, part)
     inbox[sub] = jnp.zeros((SLOT, 128), BF16)
-    peaks(z_v, gath, peak_ref)
 
     def collect(k, c):
         d = lax.rem(sub + k, SUBS)
@@ -249,6 +257,7 @@
         dma((5, 2, 4)),
         dma((SUBS,)),
         dma((SUBS,)),
+        pltpu.SemaphoreType.REGULAR,
         pltpu.SemaphoreType.REGULAR,
     ]
 

time: 37.4 us -> 36.1 us (0.965)
  Pallas kernels: 36.6 us -> 35.3 us
    pallas_call x1, Pallas kernels: 35.5 us -> 34.2 us  [body(): pl.pallas_call(kernel, out_shape=[pltpu.VMEM(s, d) for s, d in HELD], in_...]
where the time goes in v3:
time: 36.1 us; the launch traced here: 35.9 us
  Pallas kernels  35.3 us (98%)
  between operations  0.64 us (2%)
    pallas_call x1, Pallas kernels, body(): pl.pallas_call(kernel, out_shape=[pltpu.VMEM(s, d) for s, d in HELD], in_...  34.2 us
    pallas_call x1, Pallas kernels, body(): pl.pallas_call(settle, out_shape=[pltpu.HBM(s, d) for s, d in OUTS], in_s...  1.12 us

profile of v3, /device:TPU:1, one launch (start us, length us, event | category | flops | bytes accessed | tf_op | source)
XLA Modules:
  0.0 35.9 jit_solution(6384039382299606128)
XLA Ops:
  0.6 34.2 %shard_map.130 = (bf16[1,1024,256]{2,1,0:T(8,128)(2,1)S(1)}, f32[1,12,64,256]{3,2,1,0:T(8,128)S(1)}, bf16[32,24,128]{2,1,0:T(8,128)(2,1)S(1)}, bf16[256,768]{1,0:T(8,128)(2,1)S(1)}) custom-call(bf16[1,1024,1024]{2,1,0:T(8,128)(2,1)} %z_hbm.1, s32[1,64]{1,0:T(1,128)} %port_hbm.1, s32[1,64]{1,0:T(1,128)} %far_hbm.1, s32[1,64]{1,0:T(1,128)} %delay_hbm.1, ...), custom_call_target="tpu_custom_call" | custom-call | tf_op jit(solution)/shard_map/pallas_call | solution.py:270
  34.8 1.1 %shard_map.131 = (bf16[1,1024,256]{2,1,0:T(8,128)(2,1)}, f32[1,12,64,256]{3,2,1,0:T(8,128)}, f32[1,64,2,256]{3,2,1,0:T(2,128)}) custom-call(bf16[1,1024,256]{2,1,0:T(8,128)(2,1)S(1)} %get-tuple-element.7.peak, f32[1,12,64,256]{3,2,1,0:T(8,128)S(1)} %get-tuple-element.8.new, bf16[32,24,128]{2,1,0:T(8,128)(2,1)S(1)} %get-tuple-element.9.inbox, ...), custom_call_target="tpu_custom_call" | custom-call | tf_op jit(solution)/shard_map/pallas_call | solution.py:280

commit v4 on v3

--- a/solution.py
+++ b/solution.py
@@ -208,23 +208,31 @@
         peaks(z_v, gath, peak_ref, part)
     inbox[sub] = jnp.zeros((SLOT, 128), BF16)
 
-    def collect(k, c):
-        d = lax.rem(sub + k, SUBS)
+    for c in first[0] + first[1] + later:
+        c.wait_send()
+
+    def drain(k, c):
+        box(k).wait_send()
+        return c
+
+    lax.fori_loop(1, SUBS, drain, 0)
+
+    def arrived(d):
         pltpu.make_async_remote_copy(
             src_ref=outbox.at[d], dst_ref=inbox.at[d], send_sem=out_sem.at[d], recv_sem=box_sem.at[d],
             device_id=(d, blk), device_id_type=MESH).wait_recv()
+
+    arrived(chip * 2 + 1 - core)
+
+    def collect(k, c):
+        for far in (k, SUBS // 2 - k):
+            for side in range(2):
+                arrived(lax.rem(chip + far, SUBS // 2) * 2 + side)
         return c
 
-    lax.fori_loop(1, SUBS, collect, 0)
-
-    for c in first[0] + first[1] + later:
-        c.wait_send()
-
-    def drain(k, c):
-        box(k).wait_send()
-        return c
-
-    lax.fori_loop(1, SUBS, drain, 0)
+    lax.fori_loop(1, SUBS // 4, collect, 0)
+    for side in range(2):
+        arrived(lax.rem(chip + SUBS // 4, SUBS // 2) * 2 + side)
 
 
 def settle(peak, new, inbox, unpack, peak_hbm, new_hbm, arr_hbm, arr, sem):

time: 36.1 us -> 35.6 us (0.986)
  Pallas kernels: 35.3 us -> 34.8 us
    pallas_call x1, Pallas kernels: 34.2 us -> 33.6 us  [body(): pl.pallas_call(kernel, out_shape=[pltpu.VMEM(s, d) for s, d in HELD], in_...]
where the time goes in v4:
time: 35.6 us; the launch traced here: 35.4 us
  Pallas kernels  34.8 us (98%)
  between operations  0.64 us (2%)
    pallas_call x1, Pallas kernels, body(): pl.pallas_call(kernel, out_shape=[pltpu.VMEM(s, d) for s, d in HELD], in_...  33.6 us
    pallas_call x1, Pallas kernels, body(): pl.pallas_call(settle, out_shape=[pltpu.HBM(s, d) for s, d in OUTS], in_s...  1.12 us

profile of v4, /device:TPU:1, one launch (start us, length us, event | category | flops | bytes accessed | tf_op | source)
XLA Modules:
  0.0 35.4 jit_solution(14357693123302215139)
XLA Ops:
  0.6 33.6 %shard_map.130 = (bf16[1,1024,256]{2,1,0:T(8,128)(2,1)S(1)}, f32[1,12,64,256]{3,2,1,0:T(8,128)S(1)}, bf16[32,24,128]{2,1,0:T(8,128)(2,1)S(1)}, bf16[256,768]{1,0:T(8,128)(2,1)S(1)}) custom-call(bf16[1,1024,1024]{2,1,0:T(8,128)(2,1)} %z_hbm.1, s32[1,64]{1,0:T(1,128)} %port_hbm.1, s32[1,64]{1,0:T(1,128)} %far_hbm.1, s32[1,64]{1,0:T(1,128)} %delay_hbm.1, ...), custom_call_target="tpu_custom_call" | custom-call | tf_op jit(solution)/shard_map/pallas_call | solution.py:278
  34.3 1.1 %shard_map.131 = (bf16[1,1024,256]{2,1,0:T(8,128)(2,1)}, f32[1,12,64,256]{3,2,1,0:T(8,128)}, f32[1,64,2,256]{3,2,1,0:T(2,128)}) custom-call(bf16[1,1024,256]{2,1,0:T(8,128)(2,1)S(1)} %get-tuple-element.7.peak, f32[1,12,64,256]{3,2,1,0:T(8,128)S(1)} %get-tuple-element.8.new, bf16[32,24,128]{2,1,0:T(8,128)(2,1)S(1)} %get-tuple-element.9.inbox, ...), custom_call_target="tpu_custom_call" | custom-call | tf_op jit(solution)/shard_map/pallas_call | solution.py:288

commit v5 on v4

--- a/solution.py
+++ b/solution.py
@@ -82,16 +82,20 @@
     ports[...] = jnp.dot(pick, z_v[0], preferred_element_type=F32).astype(BF16)
 
 
-def waves_out(table, ports, gath, source, pack, outbox):
+def waves_out(table, ports, gath, source):
     twice = 2.0 * table[0:PB, 32:33]
     waves = []
     for t in range(2):
         volt = jnp.dot(ports[...], gath[t].reshape(1024, COLS), preferred_element_type=F32)
         wave = (twice * volt - source[t]).astype(BF16)
         waves += [wave[:, 0:128], wave[:, 128:256]]
-    stacked = jnp.concatenate(waves, axis=0)
-    boxes = jnp.dot(pack[...], stacked, preferred_element_type=F32).astype(BF16)
-    outbox[...] = boxes.reshape(SUBS, SLOT, 128)
+    return jnp.concatenate(waves, axis=0)
+
+
+def fill(part, waves, pack, outbox):
+    rows = slice(part * 8 * SLOT, part * 8 * SLOT + 8 * SLOT)
+    boxes = jnp.dot(pack[rows, :], waves, preferred_element_type=F32).astype(BF16)
+    outbox[part * 8:part * 8 + 8] = boxes.reshape(8, SLOT, 128)
 
 
 def peaks(z_v, gath, peak_ref, part):
@@ -188,7 +192,7 @@
     for c in later:
         c.wait_recv()
 
-    waves_out(table, ports, gath, source, pack, outbox)
+    waves = waves_out(table, ports, gath, source)
     pl.semaphore_wait(wide, len(WIDE))
 
     def box(k):
@@ -203,6 +207,7 @@
 
     for part in range(4):
         lo = part * 8
+        fill(part, waves, pack, outbox)
         lax.fori_loop(lo, jnp.clip(sub, lo, lo + 8), post, 0)
         lax.fori_loop(jnp.clip(sub + 1, lo, lo + 8), lo + 8, post, 0)
         peaks(z_v, gath, peak_ref, part)

time: 35.6 us -> 35.5 us (level)
  no operation moved by 1% of the time
where the time goes in v5:
time: 35.5 us; the launch traced here: 35.4 us
  Pallas kernels  34.7 us (98%)
  between operations  0.64 us (2%)
    pallas_call x1, Pallas kernels, body(): pl.pallas_call(kernel, out_shape=[pltpu.VMEM(s, d) for s, d in HELD], in_...  33.6 us
    pallas_call x1, Pallas kernels, body(): pl.pallas_call(settle, out_shape=[pltpu.HBM(s, d) for s, d in OUTS], in_s...  1.12 us

profile of v5, /device:TPU:1, one launch (start us, length us, event | category | flops | bytes accessed | tf_op | source)
XLA Modules:
  0.0 35.4 jit_solution(18271971220170411744)
XLA Ops:
  0.6 33.6 %shard_map.130 = (bf16[1,1024,256]{2,1,0:T(8,128)(2,1)S(1)}, f32[1,12,64,256]{3,2,1,0:T(8,128)S(1)}, bf16[32,24,128]{2,1,0:T(8,128)(2,1)S(1)}, bf16[256,768]{1,0:T(8,128)(2,1)S(1)}) custom-call(bf16[1,1024,1024]{2,1,0:T(8,128)(2,1)} %z_hbm.1, s32[1,64]{1,0:T(1,128)} %port_hbm.1, s32[1,64]{1,0:T(1,128)} %far_hbm.1, s32[1,64]{1,0:T(1,128)} %delay_hbm.1, ...), custom_call_target="tpu_custom_call" | custom-call | tf_op jit(solution)/shard_map/pallas_call | solution.py:283
  34.3 1.1 %shard_map.131 = (bf16[1,1024,256]{2,1,0:T(8,128)(2,1)}, f32[1,12,64,256]{3,2,1,0:T(8,128)}, f32[1,64,2,256]{3,2,1,0:T(2,128)}) custom-call(bf16[1,1024,256]{2,1,0:T(8,128)(2,1)S(1)} %get-tuple-element.7.peak, f32[1,12,64,256]{3,2,1,0:T(8,128)S(1)} %get-tuple-element.8.new, bf16[32,24,128]{2,1,0:T(8,128)(2,1)S(1)} %get-tuple-element.9.inbox, ...), custom_call_target="tpu_custom_call" | custom-call | tf_op jit(solution)/shard_map/pallas_call | solution.py:293

commit v6 on v4

--- a/solution.py
+++ b/solution.py
@@ -12,7 +12,7 @@
 CAP = 6
 SLOT = CAP * STEPS * 2
 HOPS = (1, 3, 2)
-NEAR = ((0, 1),) + tuple((k, c) for k in (1, 15, 2, 14) for c in range(2))
+NEAR = tuple((k, c) for k in (2, 14, 1, 15) for c in range(2)) + ((0, 1),)
 WIDE = ((4, 0), (12, 0))
 
 
@@ -121,6 +121,26 @@
     x = lax.rem(blk, SIDE)
     y = lax.div(blk, SIDE)
 
+    def along(axis, k):
+        if axis == 0:
+            return y, lax.rem(x + k, SIDE)
+        return lax.rem(y + k, SIDE), x
+
+    barrier = pltpu.get_barrier_semaphore()
+    for axis in range(2):
+        for k in (2, 1, 3):
+            py, px = along(axis, k)
+            pl.semaphore_signal(barrier, inc=1, device_id=(sub, py * SIDE + px), device_id_type=MESH)
+
+    chip, core = lax.div(sub, 2), lax.rem(sub, 2)
+
+    def tell(sem, offsets):
+        for k, c in offsets:
+            peer = lax.rem(chip + k, SUBS // 2) * 2 + lax.rem(core + c, 2)
+            pl.semaphore_signal(sem, inc=1, device_id=(peer, blk), device_id_type=MESH)
+
+    tell(barrier, NEAR)
+
     loads = []
     pairs = (
         (port_hbm, port_v), (far_hbm, far_v), (delay_hbm, delay_v), (adm_hbm, adm_v), (rate_hbm, rate_v),
@@ -131,26 +151,6 @@
         if n < 10:
             loads[n].start()
 
-    def along(axis, k):
-        if axis == 0:
-            return y, lax.rem(x + k, SIDE)
-        return lax.rem(y + k, SIDE), x
-
-    barrier = pltpu.get_barrier_semaphore()
-    for axis in range(2):
-        for k in HOPS:
-            py, px = along(axis, k)
-            pl.semaphore_signal(barrier, inc=1, device_id=(sub, py * SIDE + px), device_id_type=MESH)
-
-    chip, core = lax.div(sub, 2), lax.rem(sub, 2)
-
-    def tell(sem, offsets):
-        for k, c in offsets:
-            peer = lax.rem(chip + k, SUBS // 2) * 2 + lax.rem(core + c, 2)
-            pl.semaphore_signal(sem, inc=1, device_id=(peer, blk), device_id_type=MESH)
-
-    tell(barrier, NEAR)
-
     for n in range(8):
         loads[n].wait()
     turn_tables(blk, (port_v, far_v, delay_v, adm_v, rate_v, res_v), table)
@@ -161,31 +161,39 @@
 
     pl.semaphore_wait(barrier, 6 + len(NEAR))
 
-    def slab(t, yy, xx, axis, k, level):
-        ref = gath.at[t, yy, pl.ds(pl.multiple_of(xx * PB, 16), PB), :]
+    sent = []
+
+    def slab(t, yy, xx, axis, k, lo=0, size=PB):
+        n = len(sent)
+        ref = gath.at[t, yy, pl.ds(pl.multiple_of(xx * PB + lo, 16), size), :]
         py, px = along(axis, k)
         c = pltpu.make_async_remote_copy(
-            src_ref=ref, dst_ref=ref, send_sem=ring_s.at[level, t, k], recv_sem=ring_r.at[level, t, k],
+            src_ref=ref, dst_ref=ref, send_sem=ring_s.at[n], recv_sem=ring_r.at[n],
             device_id=(sub, py * SIDE + px), device_id_type=MESH)
         c.start()
+        sent.append(c)
         return c
 
-    first = [[slab(t, y, x, t, k, 0) for k in HOPS] for t in range(2)]
-    later = [slab(t, y, x, 1 - t, k, 1) for t in range(2) for k in HOPS]
-
-    tell(met, NEAR)
-    masks(far_v, table, pack, unpack)
-    for n, k in enumerate(HOPS):
+    def between():
+        tell(met, NEAR)
+        masks(far_v, table, pack, unpack)
+
+    def between2():
+        pl.semaphore_wait(met, len(NEAR))
+        tell(wide, WIDE)
+    line = {(t, k): slab(t, y, x, t, k) for k in (2, 1, 3) for t in range(2)}
+    last = [slab(t, y, x, 1 - t, j) for t in range(2) for j in (2, 1, 3)]
+    between()
+    for k in (1, 3, 2):
         for t in range(2):
-            first[t][n].wait_recv()
+            line[t, k].wait_recv()
             yy, xx = along(t, SIDE - k)
-            later += [slab(t, yy, xx, 1 - t, j, 1 + k) for j in HOPS]
-        if n == 0:
-            pl.semaphore_wait(met, len(NEAR))
-            tell(wide, WIDE)
-            loads[10].wait()
-            port_rows(table, z_v, ports)
-    for c in later:
+            last += [slab(t, yy, xx, 1 - t, j) for j in (2, 1, 3)]
+        if k == 3:
+            between2()
+    loads[10].wait()
+    port_rows(table, z_v, ports)
+    for c in last:
         c.wait_recv()
 
     waves_out(table, ports, gath, source, pack, outbox)
@@ -208,7 +216,7 @@
         peaks(z_v, gath, peak_ref, part)
     inbox[sub] = jnp.zeros((SLOT, 128), BF16)
 
-    for c in first[0] + first[1] + later:
+    for c in sent:
         c.wait_send()
 
     def drain(k, c):
@@ -261,8 +269,8 @@
         pltpu.VMEM((SUBS, SLOT, 128), BF16),
         pltpu.VMEM((SUBS * SLOT, 256), BF16),
         dma((len(args),)),
-        dma((5, 2, 4)),
-        dma((5, 2, 4)),
+        dma((40,)),
+        dma((40,)),
         dma((SUBS,)),
         dma((SUBS,)),
         pltpu.SemaphoreType.REGULAR,

time: 35.6 us -> 35.5 us (level)
  no operation moved by 1% of the time
where the time goes in v6:
time: 35.5 us; the launch traced here: 35.4 us
  Pallas kernels  34.7 us (98%)
  between operations  0.64 us (2%)
    pallas_call x1, Pallas kernels, body(): pl.pallas_call(kernel, out_shape=[pltpu.VMEM(s, d) for s, d in HELD], in_...  33.6 us
    pallas_call x1, Pallas kernels, body(): pl.pallas_call(settle, out_shape=[pltpu.HBM(s, d) for s, d in OUTS], in_s...  1.12 us

profile of v6, /device:TPU:1, one launch (start us, length us, event | category | flops | bytes accessed | tf_op | source)
XLA Modules:
  0.0 35.4 jit_solution(7488737547549149758)
XLA Ops:
  0.6 33.6 %shard_map.130 = (bf16[1,1024,256]{2,1,0:T(8,128)(2,1)S(1)}, f32[1,12,64,256]{3,2,1,0:T(8,128)S(1)}, bf16[32,24,128]{2,1,0:T(8,128)(2,1)S(1)}, bf16[256,768]{1,0:T(8,128)(2,1)S(1)}) custom-call(bf16[1,1024,1024]{2,1,0:T(8,128)(2,1)} %z_hbm.1, s32[1,64]{1,0:T(1,128)} %port_hbm.1, s32[1,64]{1,0:T(1,128)} %far_hbm.1, s32[1,64]{1,0:T(1,128)} %delay_hbm.1, ...), custom_call_target="tpu_custom_call" | custom-call | tf_op jit(solution)/shard_map/pallas_call | solution.py:286
  34.3 1.1 %shard_map.131 = (bf16[1,1024,256]{2,1,0:T(8,128)(2,1)}, f32[1,12,64,256]{3,2,1,0:T(8,128)}, f32[1,64,2,256]{3,2,1,0:T(2,128)}) custom-call(bf16[1,1024,256]{2,1,0:T(8,128)(2,1)S(1)} %get-tuple-element.7.peak, f32[1,12,64,256]{3,2,1,0:T(8,128)S(1)} %get-tuple-element.8.new, bf16[32,24,128]{2,1,0:T(8,128)(2,1)S(1)} %get-tuple-element.9.inbox, ...), custom_call_target="tpu_custom_call" | custom-call | tf_op jit(solution)/shard_map/pallas_call | solution.py:296
